TPU v7x, 256 devices: a whole 4x4x8 slice. The times are simulated.
256 devices in a mesh: dp: 8 (over y, core), tensor: 32 (over x, z).
Axes of the slice: x: 4, y: 4, z: 8, core: 2. Of those that a mesh axis runs over, the one named last changes fastest.
Arguments:
- hidden: bfloat16 [8192, 2048], P(('dp', 'tensor')), parts along dimension 0, may hold values from -6 to 6
- norm_gain: bfloat16 [2048], replicated, may hold values from 0.099609375 to 1.8984375
- router_weight: bfloat16 [2048, 8], replicated, may hold values from -0.125 to 0.125
- kv_weight: bfloat16 [2048, 4096], P(None, 'tensor'), may hold values from -0.125 to 0.125
- query_weight: bfloat16 [2048, 16384], P(None, 'tensor'), may hold values from -0.125 to 0.125
- out_weight: bfloat16 [16384, 2048], P('tensor'), may hold values from -0.5 to 0.5
- routes: int32 [8192, 2], P('dp'), parts along dimension 0, may hold values from 0 to 7, all different within a row; in each aligned block of 1024 rows (0 to 1023, 1024 to 2047, ...) at most 384 rows name the same one
- segment_ids: int32 [8192], P('dp'), parts along dimension 0, may hold values from 0 to 3, never falling along the last dimension, each value on 1 to 512 neighbouring positions
- page_table: int32 [64], P('dp'), parts along dimension 0, may hold values from 0 to 15, as said below
- kv_cache: bfloat16 [128, 128, 4096], P('dp', None, 'tensor'), parts along dimension 0, may hold values from -6 to 6
Outputs:
- attended_out: bfloat16 [8192, 2048], P(('dp', 'tensor')), parts along dimension 0
- new_cache: bfloat16 [128, 128, 4096], P('dp', None, 'tensor'), parts along dimension 0
There are 8 independent parts, one for each index of `dp`. A program takes and returns all parts, laid end to end along the dimension named above; an argument that names none is the same for every part. Nothing has to cross between parts.
Inputs may be any that keep to these rules, and one draw needn't show every extreme that they name: `routes`: no expert is named by more than 384 tokens of a batch, and one is named by exactly 384; a token names two different experts. `segment_ids`: ids never fall along the pack; each prompt has 1 to 512 tokens and one has exactly 512. `page_table`: distinct pages.
All inputs are finite; a program needn't handle non-finite values.
Results may differ from a plain program's by a relative error of at most 0.025.
Values may be sent and summed in bfloat16 or wider, within the bound.
A program may use at most 128 MiB of HBM per device.

v0:
```python
import jax
import jax.numpy as jnp
from jax import lax
from jax.sharding import PartitionSpec as P

D = 2048
HD = 128
EA = 8
PAGE = 128


def swapped(array, axis, bit):
    return lax.ppermute(array, axis, [(i, i ^ 1 << bit) for i in range(lax.axis_size(axis))])


def normalize(hidden, norm_gain):
    values = hidden.astype(jnp.float32)
    factor = lax.rsqrt(jnp.mean(values * values, axis=-1, keepdims=True) + 1e-05)
    return (values * factor * norm_gain.astype(jnp.float32)).astype(jnp.bfloat16)


def gate_table(normed, router_weight, routes):
    logits = jnp.dot(normed, router_weight, preferred_element_type=jnp.float32)
    chosen = jnp.take_along_axis(logits, routes, axis=1)
    weights = jax.nn.softmax(chosen, axis=-1)
    expert_ids = jnp.arange(router_weight.shape[1], dtype=jnp.int32)
    onehot = (routes[:, :, None] == expert_ids[None, None, :]).astype(jnp.float32)
    return jnp.sum(weights[:, :, None] * onehot, axis=1)


def positions_of(segment_ids):
    index_row = jnp.arange(segment_ids.shape[0], dtype=jnp.int32)
    starts_here = jnp.concatenate([jnp.ones((1,), dtype=bool), segment_ids[1:] != segment_ids[:-1]])
    segment_start = lax.cummax(jnp.where(starts_here, index_row, 0), axis=0)
    return index_row - segment_start


def rotate(values, positions):
    half_width = values.shape[-1] // 2
    frequency = 10000.0 ** (-jnp.arange(half_width, dtype=jnp.float32) / half_width)
    angles = positions.astype(jnp.float32)[:, None] * frequency[None, :]
    angles = angles.reshape((values.shape[0],) + (1,) * (values.ndim - 2) + (half_width,))
    cosine = jnp.cos(angles)
    sine_part = jnp.sin(angles)
    leading = values[..., :half_width]
    trailing = values[..., half_width:]
    return jnp.concatenate(
        [leading * cosine - trailing * sine_part, trailing * cosine + leading * sine_part], axis=-1
    )


def expert_slots(routes, expert, capacity):
    is_hit = jnp.any(routes == expert, axis=1)
    running = jnp.cumsum(is_hit.astype(jnp.int32))
    placed = jnp.where(is_hit, running - 1, capacity)
    index_row = jnp.arange(routes.shape[0], dtype=jnp.int32)
    slot_tok = jnp.zeros((capacity + 1,), jnp.int32).at[placed].set(index_row)[:capacity]
    is_valid = jnp.arange(capacity, dtype=jnp.int32) < running[-1]
    return (slot_tok, is_valid)


def attend(queries, key_rows, value_rows, allowed):
    scores = jnp.dot(queries, key_rows.T, preferred_element_type=jnp.float32)
    scores = jnp.where(allowed, scores, -1e30)
    probabilities = jax.nn.softmax(scores, axis=-1).astype(jnp.bfloat16)
    return jnp.dot(probabilities, value_rows, preferred_element_type=jnp.float32)


def project_kv(normed, weight, positions, first_block):
    projected = jnp.dot(normed, weight, preferred_element_type=jnp.float32)
    block_total = weight.shape[1] // HD
    blocks = projected.reshape(normed.shape[0], block_total, HD)
    block_index = first_block + jnp.arange(block_total, dtype=jnp.int32)
    turned = rotate(blocks, positions)
    chosen = jnp.where((block_index % 2 == 0)[None, :, None], turned, blocks)
    return chosen.astype(jnp.bfloat16).reshape(normed.shape[0], weight.shape[1])


def local(
    hidden,
    norm_gain,
    router_weight,
    kv_weight,
    query_weight,
    out_weight,
    routes,
    segment_ids,
    page_table,
    kv_cache,
):
    device_index = lax.axis_index("tensor")
    token_count = routes.shape[0]
    capacity = 3 * token_count // 8
    normed = lax.all_gather(normalize(hidden, norm_gain), "tensor", axis=0, tiled=True)
    gates = gate_table(normed, router_weight, routes)
    positions = positions_of(segment_ids)
    kv_width = kv_weight.shape[1]
    block_count = kv_width // HD
    own_rows = project_kv(normed, kv_weight, positions, device_index * block_count)
    new_cache = kv_cache.at[page_table].set(own_rows.reshape(page_table.shape[0], PAGE, kv_width))
    partner_rows = swapped(own_rows, "tensor", 0)
    leading_first = device_index % 2 == 0
    head_rows = jnp.where(
        leading_first,
        jnp.concatenate([own_rows, partner_rows], axis=1),
        jnp.concatenate([partner_rows, own_rows], axis=1),
    )
    local_heads = head_rows.shape[1] // (2 * HD)
    head_rows = head_rows.reshape(token_count, local_heads, 2, HD)
    pair_count = query_weight.shape[1] // HD
    local_experts = pair_count // local_heads
    query_cols = query_weight.reshape(D, local_heads, local_experts, HD)
    index_row = jnp.arange(token_count, dtype=jnp.int32)
    scale_factor = HD ** (-0.5)
    spread = jnp.zeros((token_count, local_heads, local_experts, HD), jnp.bfloat16)
    for expert_slot in range(local_experts):
        expert = (device_index * pair_count + expert_slot) % EA
        slot_tok, is_valid = expert_slots(routes, expert, capacity)
        queries = jnp.einsum(
            "cd,dhk->chk",
            normed[slot_tok],
            query_cols[:, :, expert_slot],
            preferred_element_type=jnp.float32,
        )
        queries = (rotate(queries, positions[slot_tok]) * scale_factor).astype(jnp.bfloat16)
        allowed = (segment_ids[slot_tok][:, None] == segment_ids[None, :]) & (
            index_row[None, :] <= slot_tok[:, None]
        )
        attended = jnp.stack(
            [attend(queries[:, 0], head_rows[:, 0, 0], head_rows[:, 0, 1], allowed)], axis=1
        )
        gate_here = gates[slot_tok, expert] * is_valid.astype(jnp.float32)
        gated = (attended * gate_here[:, None, None]).astype(jnp.bfloat16)
        target = jnp.where(is_valid, slot_tok, token_count)
        spread = spread.at[target, :, expert_slot].set(gated, mode="drop")
    flat_spread = spread.reshape(token_count, pair_count * HD)
    reduced = lax.psum_scatter(
        jnp.dot(flat_spread, out_weight, preferred_element_type=jnp.float32).astype(jnp.bfloat16),
        "tensor",
        scatter_dimension=0,
        tiled=True,
    ).astype(jnp.float32)
    attended_out = (hidden.astype(jnp.float32) + reduced).astype(jnp.bfloat16)
    return (attended_out, new_cache)


def solution(mesh):
    placed = (
        P(("dp", "tensor"), None),
        P(),
        P(),
        P(None, "tensor"),
        P(None, "tensor"),
        P("tensor", None),
        P("dp", None),
        P("dp"),
        P("dp"),
        P("dp", None, "tensor"),
    )
    return jax.shard_map(
        local,
        mesh=mesh,
        in_specs=placed,
        out_specs=(P(("dp", "tensor"), None), P("dp", None, "tensor")),
        check_vma=False,
    )
```

profile of v0, /device:TPU:8, one launch (start us, length us, event | category | flops | bytes accessed | tf_op | source)
XLA Modules:
  0.0 492.1 jit_solution(13262688912807085128)
XLA Ops:
  7.2 0.8 convert_element_type.154
  8.1 1.0 fusion.27
  9.1 1.7 fusion.29
  12.7 0.7 slice.143
  14.0 4.3 scatter_custom_fusion.6
  18.3 1.1 shift-left_or_fusion
  19.4 3.0 gather_fusion.12
  22.6 1.9 gather_fusion.14
  24.5 4.3 scatter_custom_fusion.4
  28.8 1.3 shift-left_or_fusion.1
  30.1 1.9 gather_fusion.10
  32.0 3.0 gather_fusion.8
  36.0 0.6 slice.136
  36.9 4.3 scatter_custom_fusion.2
  41.2 1.2 shift-left_or_fusion.2
  42.4 1.9 gather_fusion.6
  44.3 3.0 gather_fusion.4
  47.4 0.6 slice.121
  48.0 4.8 scatter_custom_fusion
  52.7 1.2 shift-left_or_fusion.3
  54.0 1.9 gather_fusion.2
  55.9 3.0 gather_fusion
  58.9 3.9 copy.62
  62.8 0.6 convert_element_type.172
  63.4 0.6 convert_element_type.179
  64.0 0.6 convert_element_type.165
  65.7 0.6 fusion.81
  66.3 0.6 fusion.83
  66.9 0.6 fusion.85
  67.5 0.6 fusion.87
  68.1 27.8 %all-gather.2.cloned.1.call-done = bf16[1024,2048]{1,0:T(8,128)(2,1)} async-done(((bf16[32,2048]{1,0:T(8,128)(2,1)}), bf16[1024,2048]{1,0:T(8,128)(2,1)}) %all-gather.2.cloned.1.call-update) | async-done | bytes 4194320 | tf_op jit(solution)/shard_map/all_gather | solution.py:94
  95.9 7.8 %gather_fusion.13 = bf16[384,2048]{1,0:T(8,128)(2,1)} fusion(bf16[1024,2048]{1,0:T(8,128)(2,1)} %all-gather.2.cloned.1.call-done, s32[1024]{0:T(1024)S(1)} %pad_clamp_fusion), kind=kCustom, calls=%fused_computation.13 | custom fusion | bytes 3147264 | tf_op jit(solution)/shard_map/gather | solution.py:121
  103.7 2.8 convolution_bitcast_fusion
  106.5 7.8 %gather_fusion.9 = bf16[384,2048]{1,0:T(8,128)(2,1)} fusion(bf16[1024,2048]{1,0:T(8,128)(2,1)} %all-gather.2.cloned.1.call-done, s32[1024]{0:T(1024)S(1)} %pad_clamp_fusion.1), kind=kCustom, calls=%fused_computation.9 | custom fusion | bytes 3147264 | tf_op jit(solution)/shard_map/gather | solution.py:121
  114.2 2.9 convolution_bitcast_fusion.1
  117.1 3.9 fusion.110
  121.0 1.2 fusion.24
  122.2 0.8 fusion.18
  122.9 1.9 collective-permute-start
  124.9 1.2 fusion.111
  126.0 12.5 %gather_fusion.16 = f32[2048]{0:T(1024)S(1)} fusion(f32[1024,8]{0,1:T(8,128)S(1)} %fusion.111, s32[2048]{0:T(1024)S(1)} %reshape.1033), kind=kCustom, calls=%fused_computation.16 | custom fusion | bytes 32768 | tf_op jit(solution)/shard_map/jit(take_along_axis)/gather | solution.py:24
  139.4 2.7 gather_fusion.15
  142.6 2.7 gather_fusion.11
  145.3 0.7 fusion.78
  146.0 2.7 gather_fusion.7
  148.7 0.6 fusion.79
  149.4 7.8 %gather_fusion.1 = bf16[384,2048]{1,0:T(8,128)(2,1)} fusion(bf16[1024,2048]{1,0:T(8,128)(2,1)} %all-gather.2.cloned.1.call-done, s32[1024]{0:T(1024)S(1)} %copy-done.24), kind=kCustom, calls=%fused_computation.1 | custom fusion | bytes 3147264 | tf_op jit(solution)/shard_map/gather | solution.py:121
  157.1 2.1 convolution_bitcast_fusion.3
  159.3 2.7 gather_fusion.3
  162.0 0.6 fusion.80
  163.1 7.8 %gather_fusion.5 = bf16[384,2048]{1,0:T(8,128)(2,1)} fusion(bf16[1024,2048]{1,0:T(8,128)(2,1)} %all-gather.2.cloned.1.call-done, s32[1024]{0:T(1024)S(1)} %copy-done.22), kind=kCustom, calls=%fused_computation.5 | custom fusion | bytes 3147264 | tf_op jit(solution)/shard_map/gather | solution.py:121
  170.9 2.2 convolution_bitcast_fusion.2
  173.1 1.5 fusion.52
  174.7 1.4 maximum_select_fusion.1
  183.0 19.2 %scatter_fusion = bf16[1024,4,128]{2,1,0:T(4,128)(2,1)S(1)} fusion(bf16[1024,4,128]{2,1,0:T(4,128)(2,1)S(1)} %broadcast.766, s32[384]{0:T(512)S(1)} %copy-done.7, bf16[384,128]{1,0:T(8,128)(2,1)S(1)} %fusion.12), kind=kCustom, calls=%fused_computation.18 | custom fusion | bytes 297984 | tf_op jit(solution)/shard_map/scatter | solution.py:135
  202.2 19.7 %scatter_fusion.1 = bf16[1024,4,128]{2,1,0:T(4,128)(2,1)S(1)} fusion(bf16[1024,4,128]{2,1,0:T(4,128)(2,1)S(1)} %scatter_fusion, s32[384]{0:T(512)S(1)} %copy-done.6, bf16[384,128]{1,0:T(8,128)(2,1)S(1)} %fusion.13), kind=kCustom, calls=%fused_computation.20 | custom fusion | bytes 297984 | tf_op jit(solution)/shard_map/scatter | solution.py:135
  221.9 19.7 %scatter_fusion.2 = bf16[1024,4,128]{2,1,0:T(4,128)(2,1)S(1)} fusion(bf16[1024,4,128]{2,1,0:T(4,128)(2,1)S(1)} %scatter_fusion.1, s32[384]{0:T(512)S(1)} %copy-done.5, bf16[384,128]{1,0:T(8,128)(2,1)S(1)} %fusion.14), kind=kCustom, calls=%fused_computation.22 | custom fusion | bytes 297984 | tf_op jit(solution)/shard_map/scatter | solution.py:135
  241.6 19.6 %scatter_fusion.3 = bf16[1024,4,128]{2,1,0:T(4,128)(2,1)S(1)} fusion(bf16[1024,4,128]{2,1,0:T(4,128)(2,1)S(1)} %scatter_fusion.2, s32[384]{0:T(512)S(1)} %copy-done.4, bf16[384,128]{1,0:T(8,128)(2,1)S(1)} %fusion.15), kind=kCustom, calls=%fused_computation.24 | custom fusion | bytes 297984 | tf_op jit(solution)/shard_map/scatter | solution.py:135
  261.2 4.3 convolution_convert_fusion
  265.5 0.6 copy-done.39
  266.1 1.1 copy.70
  267.3 0.8 scatter_fusion.4
  268.1 215.4 %reduce-scatter.2.cloned.1.call-done = bf16[32,2048]{1,0:T(8,128)(2,1)} async-done(((bf16[1024,2048]{1,0:T(8,128)(2,1)}), bf16[32,2048]{1,0:T(8,128)(2,1)}) %reduce-scatter.2.cloned.1.call-update) | async-done | bytes 131088 | tf_op jit(solution)/shard_map/reduce_scatter | solution.py:137
  483.4 1.6 fusion.30
  (155 shorter events, 13.5 us)
Async XLA Ops:
  7.2 254.0 %copy-start = (bf16[512,2048]{1,0:T(8,128)(2,1)S(1)}, bf16[512,2048]{1,0:T(8,128)(2,1)}, u32[]{:S(2)}) copy-start(bf16[512,2048]{1,0:T(8,128)(2,1)} %param.15) | copy-start | bytes 6291460
  7.2 3.7 copy-start.18
  7.2 6.2 %copy-start.1 = (s32[1024]{0:T(1024)S(1)}, s32[1024]{0:T(1024)}, u32[]{:S(2)}) copy-start(s32[1024]{0:T(1024)} %param.17) | copy-start | bytes 12292
  7.2 88.7 %all-gather.2.cloned.1.call-start = ((), (), s32[]{:S(2)}) async-start(), calls=%async_computation.1 | async-start | bytes 4325376 | tf_op jit(solution)/shard_map/all_gather | solution.py:94
  10.8 472.6 %reduce-scatter.2.cloned.1.call-start = ((), (), s32[]{:S(2)}) async-start(), calls=%async_computation.2 | async-start | bytes 4325376 | tf_op jit(solution)/shard_map/reduce_scatter | solution.py:137
  42.4 4.9 %copy-start.21 = (s32[1024]{0:T(1024)}, s32[1024]{0:T(1024)S(1)}, u32[]{:S(2)}) copy-start(s32[1024]{0:T(1024)S(1)} %pad_clamp_fusion.2) | copy-start | bytes 12292
  54.0 4.9 copy-start.23
  68.1 52.9 %copy-start.29 = (f32[64]{0:T(128)}, f32[64]{0:T(128)S(1)}, u32[]{:S(2)}) copy-start(f32[64]{0:T(128)S(1)} %multiply_power_fusion) | copy-start | bytes 772
  114.2 2.9 copy-start.15
  117.1 7.7 %copy-start.3 = (bf16[1024,2048]{1,0:T(8,128)(2,1)S(1)}, bf16[1024,2048]{1,0:T(8,128)(2,1)}, u32[]{:S(2)}) copy-start(bf16[1024,2048]{1,0:T(8,128)(2,1)} %all-gather.2.cloned.1.call-done) | copy-start | bytes 12582916
  121.0 3.9 copy-start.20
  122.9 51.7 %collective-permute-start = (bf16[1024,128]{0,1:T(8,128)(2,1)}, bf16[1024,128]{0,1:T(8,128)(2,1)}, u32[]{:S(2)}, u32[]{:S(2)}) collective-permute-start(bf16[1024,128]{0,1:T(8,128)(2,1)} %fusion.18), channel_id=1, source_target_pairs={{0,1},{1,0},{2,3},{3,2},{4,5},{5,4},{6,7},{7,6},{8,9},{9,8},{10,11... | collective-permute-start | bytes 786440 | tf_op jit(solution)/shard_map/ppermute | solution.py:13
  126.0 13.2 %copy-start.19 = (s32[1024,2]{0,1:T(2,128)S(1)}, s32[1024,2]{0,1:T(2,128)}, u32[]{:S(2)}) copy-start(s32[1024,2]{0,1:T(2,128)} %param.16) | copy-start | bytes 24580
  126.0 13.3 %copy-start.8 = (s32[384]{0:T(512)S(1)}, s32[384]{0:T(512)}, u32[]{:S(2)}) copy-start(s32[384]{0:T(512)} %get-tuple-element.28) | copy-start | bytes 4612
  139.0 3.6 copy-start.9
  142.1 4.0 copy-start.10
  145.3 4.0 copy-start.24
  157.1 2.1 copy-start.11
  159.3 3.4 copy-start.28
  159.3 3.4 copy-start.30
  159.3 3.8 copy-start.22
  170.9 2.2 copy-start.16
  170.9 2.2 copy-start.17
  170.9 2.2 copy-start.25
  170.9 2.2 copy-start.26
  170.9 2.2 copy-start.27
  173.1 3.0 copy-start.2
  173.1 3.0 copy-start.31
  173.1 3.0 copy-start.35
  177.1 0.7 copy-start.32
  177.1 0.7 copy-start.36
  178.8 0.7 copy-start.33
  178.8 0.7 copy-start.37
  180.5 0.7 copy-start.34
  180.5 0.7 copy-start.38
  182.2 0.8 copy-start.7
  182.7 19.5 %copy-start.6 = (s32[384]{0:T(512)S(1)}, s32[384]{0:T(512)}, u32[]{:S(2)}) copy-start(s32[384]{0:T(512)} %fusion.83) | copy-start | bytes 4612
  183.0 38.9 %copy-start.5 = (s32[384]{0:T(512)S(1)}, s32[384]{0:T(512)}, u32[]{:S(2)}) copy-start(s32[384]{0:T(512)} %fusion.85) | copy-start | bytes 4612
  202.2 39.4 %copy-start.4 = (s32[384]{0:T(512)S(1)}, s32[384]{0:T(512)}, u32[]{:S(2)}) copy-start(s32[384]{0:T(512)} %fusion.87) | copy-start | bytes 4612
  265.5 0.7 copy-start.39
  265.5 1.8 copy-start.14
  265.5 218.0 %copy-start.12 = (bf16[32,2048]{1,0:T(8,128)(2,1)S(1)}, bf16[32,2048]{1,0:T(8,128)(2,1)}, u32[]{:S(2)}) copy-start(bf16[32,2048]{1,0:T(8,128)(2,1)} %param.10) | copy-start | bytes 393220
  268.1 217.0 %copy-start.13 = (bf16[16,128,128]{2,1,0:T(8,128)(2,1)}, bf16[16,128,128]{2,1,0:T(8,128)(2,1)S(1)}, u32[]{:S(2)}) copy-start(bf16[16,128,128]{2,1,0:T(8,128)(2,1)S(1)} %scatter_fusion.4) | copy-start | bytes 1572868
Sparse Core Ops, SparseCore 0:
  11.2 84.6 all-gather.1
  265.6 217.7 reduce-scatter.1
where the time goes:
time: 498 us; the launch traced here: 492 us
  waiting for transfers between devices  243 us (49%)
  local copies, waits for them, and re-layouts  182 us (37%)
  other arithmetic  26.6 us (5%)
  matrix products  23.4 us (5%)
  between operations  15.1 us (3%)
    reduce_scatter x1, waiting for transfers between devices, local(): lax.psum_scatter(jnp.dot(flat_spread, out_weight, preferred_element_type=...  215 us
    scatter x4, local copies, waits for them, and re-layouts, local(): spread = spread.at[target, :, expert_slot].set(gated, mode='drop')  78.1 us
    gather x4, local copies, waits for them, and re-layouts, local(): normed[slot_tok]  31.1 us
    all_gather x1, waiting for transfers between devices, local(): lax.all_gather(normalize(hidden, norm_gain), 'tensor', axis=0, tiled=True)  27.8 us
    scatter x4, local copies, waits for them, and re-layouts, expert_slots(): jnp.zeros((capacity + 1,), jnp.int32).at[placed].set(index_row)[:capacity]  17.7 us
    gather x5, local copies, waits for them, and re-layouts, gate_table(): chosen = jnp.take_along_axis(logits, routes, axis=1)  13.7 us
    gather x4, local copies, waits for them, and re-layouts, local(): segment_ids[slot_tok][:, None] == segment_ids[None, :]  12.1 us
    gather x4, local copies, waits for them, and re-layouts, local(): gate_here = gates[slot_tok, expert] * is_valid.astype(jnp.float32)  10.7 us
  transfers between devices with their start and end apart: 3, of which 2 were waited for; matrix products, arithmetic and copies ran while one was open for 22% of the time, Pallas kernels for 0%

commit v1 on v0

--- a/solution.py
+++ b/solution.py
@@ -88,10 +88,19 @@
     page_table,
     kv_cache,
 ):
+
+    def lead_frame(xin):
+        ledger = []
+        dev_count = lax.psum(1, "tensor")
+        for ix in range(xin.ndim):
+            ledger.append(dev_count if ix == 0 else 1)
+        upper = jnp.tile(xin, ledger)
+        return lax.all_to_all(upper, "tensor", split_axis=0, concat_axis=0, tiled=True)
+
     device_index = lax.axis_index("tensor")
     token_count = routes.shape[0]
     capacity = 3 * token_count // 8
-    normed = lax.all_gather(normalize(hidden, norm_gain), "tensor", axis=0, tiled=True)
+    normed = lead_frame(normalize(hidden, norm_gain))
     gates = gate_table(normed, router_weight, routes)
     positions = positions_of(segment_ids)
     kv_width = kv_weight.shape[1]

time: 498 us -> 535 us (1.074)
  local copies, waits for them, and re-layouts: 182 us -> 195 us
  waiting for transfers between devices: 243 us -> 256 us
  starting transfers between devices: 1.99 us -> 11.7 us
    all_to_all x0 -> x1, waiting for transfers between devices: none -> 40.2 us  [lead_frame(): lax.all_to_all(upper, 'tensor', split_axis=0, concat_axis=0, tiled=True)]
    all_gather x1 -> x0, waiting for transfers between devices: 27.8 us -> none  [local(): lax.all_gather(normalize(hidden, norm_gain), 'tensor', axis=0, tiled=True)]
    all_to_all x0 -> x1, starting transfers between devices: none -> 11.6 us  [lead_frame(): lax.all_to_all(upper, 'tensor', split_axis=0, concat_axis=0, tiled=True)]
    gather x4, local copies, waits for them, and re-layouts: 31.1 us -> 41.8 us  [local(): normed[slot_tok]]
  transfers between devices with their start and end apart: 3 -> 3, of which waited for: 2 -> 2; matrix products, arithmetic and copies ran while one was open for 22% -> 18% of each run, Pallas kernels for 0% -> 0%
where the time goes in v1:
time: 535 us; the launch traced here: 528 us
  waiting for transfers between devices  256 us (48%)
  local copies, waits for them, and re-layouts  195 us (36%)
  other arithmetic  25.7 us (5%)
  matrix products  24.5 us (5%)
  between operations  15.1 us (3%)
  starting transfers between devices  11.7 us (2%)
    reduce_scatter x1, waiting for transfers between devices, local(): lax.psum_scatter(jnp.dot(flat_spread, out_weight, preferred_element_type=...  216 us
    scatter x4, local copies, waits for them, and re-layouts, local(): spread = spread.at[target, :, expert_slot].set(gated, mode='drop')  78.1 us
    gather x4, local copies, waits for them, and re-layouts, local(): normed[slot_tok]  41.8 us
    all_to_all x1, waiting for transfers between devices, lead_frame(): lax.all_to_all(upper, 'tensor', split_axis=0, concat_axis=0, tiled=True)  40.2 us
    scatter x4, local copies, waits for them, and re-layouts, expert_slots(): jnp.zeros((capacity + 1,), jnp.int32).at[placed].set(index_row)[:capacity]  17.6 us
    gather x5, local copies, waits for them, and re-layouts, gate_table(): chosen = jnp.take_along_axis(logits, routes, axis=1)  13.7 us
    gather x4, local copies, waits for them, and re-layouts, local(): segment_ids[slot_tok][:, None] == segment_ids[None, :]  11.9 us
    all_to_all x1, starting transfers between devices, lead_frame(): lax.all_to_all(upper, 'tensor', split_axis=0, concat_axis=0, tiled=True)  11.6 us
  transfers between devices with their start and end apart: 3, of which 2 were waited for; matrix products, arithmetic and copies ran while one was open for 18% of the time, Pallas kernels for 0%

profile of v1, /device:TPU:8, one launch (start us, length us, event | category | flops | bytes accessed | tf_op | source)
XLA Modules:
  0.0 528.0 jit_solution(5204524239605948430)
XLA Ops:
  7.2 0.8 convert_element_type.154
  8.0 1.0 fusion.27
  9.1 1.0 fusion.29
  10.1 2.5 tile.2
  12.6 11.6 %all-to-all-start = ((bf16[32,32,2048]{2,1,0:T(8,128)(2,1)}), bf16[32,32,2048]{2,1,0:T(8,128)(2,1)}, u32[]{:S(2)}, u32[]{:S(2)}) async-start(bf16[32,32,2048]{2,1,0:T(8,128)(2,1)} %tile.2), calls=%async_computation | async-start | bytes 8388608 | tf_op jit(solution)/shard_map/all_to_all | solution.py:98
  25.3 0.6 slice.150
  26.1 0.7 slice.143
  27.3 4.3 scatter_custom_fusion.6
  31.7 1.2 shift-left_or_fusion
  32.9 3.0 gather_fusion.12
  36.1 1.9 gather_fusion.14
  38.0 4.3 scatter_custom_fusion.4
  42.3 1.3 shift-left_or_fusion.1
  43.6 1.9 gather_fusion.10
  45.5 2.9 gather_fusion.8
  49.4 0.6 slice.136
  50.2 4.3 scatter_custom_fusion.2
  54.5 1.2 shift-left_or_fusion.2
  55.8 1.9 gather_fusion.6
  57.6 3.0 gather_fusion.4
  61.2 4.7 scatter_custom_fusion
  65.9 1.2 shift-left_or_fusion.3
  67.0 1.9 gather_fusion.2
  68.9 3.0 gather_fusion
  71.9 4.0 copy.62
  75.9 0.6 convert_element_type.172
  76.5 0.6 convert_element_type.179
  78.2 0.6 convert_element_type.156
  79.9 0.6 fusion.85
  80.5 0.6 fusion.87
  81.1 40.2 %all-to-all-done = bf16[32,32,2048]{2,1,0:T(8,128)(2,1)} async-done(((bf16[32,32,2048]{2,1,0:T(8,128)(2,1)}), bf16[32,32,2048]{2,1,0:T(8,128)(2,1)}, u32[]{:S(2)}, u32[]{:S(2)}) %all-to-all-start) | async-done | bytes 4194336 | tf_op jit(solution)/shard_map/all_to_all | solution.py:98
  121.4 7.8 %gather_fusion.13 = bf16[384,2048]{1,0:T(8,128)(2,1)} fusion(bf16[1024,2048]{1,0:T(8,128)(2,1)} %bitcast.5, s32[1024]{0:T(1024)S(1)} %pad_clamp_fusion), kind=kCustom, calls=%fused_computation.13 | custom fusion | bytes 3147264 | tf_op jit(solution)/shard_map/gather | solution.py:130
  129.1 7.8 %gather_fusion.9 = bf16[384,2048]{1,0:T(8,128)(2,1)} fusion(bf16[1024,2048]{1,0:T(8,128)(2,1)} %bitcast.5, s32[1024]{0:T(1024)S(1)} %pad_clamp_fusion.1), kind=kCustom, calls=%fused_computation.9 | custom fusion | bytes 3147264 | tf_op jit(solution)/shard_map/gather | solution.py:130
  137.0 7.8 %gather_fusion.5 = bf16[384,2048]{1,0:T(8,128)(2,1)} fusion(bf16[1024,2048]{1,0:T(8,128)(2,1)} %bitcast.5, s32[1024]{0:T(1024)S(1)} %pad_clamp_fusion.2), kind=kCustom, calls=%fused_computation.5 | custom fusion | bytes 3147264 | tf_op jit(solution)/shard_map/gather | solution.py:130
  144.8 18.4 %gather_fusion.1 = bf16[384,2048]{1,0:T(8,128)(2,1)} fusion(bf16[1024,2048]{1,0:T(8,128)(2,1)} %bitcast.5, s32[1024]{0:T(1024)S(1)} %pad_clamp_fusion.3), kind=kCustom, calls=%fused_computation.1 | custom fusion | bytes 3147264 | tf_op jit(solution)/shard_map/gather | solution.py:130
  163.1 2.9 convolution_bitcast_fusion
  166.0 2.4 convolution_bitcast_fusion.1
  168.4 3.7 fusion.110
  172.2 1.2 fusion.24
  173.3 0.8 fusion.18
  174.1 3.4 fusion.111
  177.5 12.5 %gather_fusion.16 = f32[2048]{0:T(1024)S(1)} fusion(f32[1024,8]{0,1:T(8,128)S(1)} %fusion.111, s32[2048]{0:T(1024)S(1)} %reshape.1040), kind=kCustom, calls=%fused_computation.16 | custom fusion | bytes 32768 | tf_op jit(solution)/shard_map/jit(take_along_axis)/gather | solution.py:24
  190.8 2.7 gather_fusion.15
  193.5 0.6 fusion.77
  194.2 2.7 gather_fusion.11
  196.9 0.7 fusion.78
  197.6 2.7 gather_fusion.7
  200.3 0.6 fusion.79
  200.9 2.7 gather_fusion.3
  203.6 0.7 fusion.80
  204.3 2.1 convolution_bitcast_fusion.3
  207.0 1.6 convolution_bitcast_fusion.2
  208.7 1.3 fusion.52
  210.0 1.4 maximum_select_fusion.1
  218.2 19.2 %scatter_fusion = bf16[1024,4,128]{2,1,0:T(4,128)(2,1)S(1)} fusion(bf16[1024,4,128]{2,1,0:T(4,128)(2,1)S(1)} %broadcast.769, s32[384]{0:T(512)S(1)} %copy-done.6, bf16[384,128]{1,0:T(8,128)(2,1)S(1)} %fusion.12), kind=kCustom, calls=%fused_computation.18 | custom fusion | bytes 297984 | tf_op jit(solution)/shard_map/scatter | solution.py:144
  237.4 19.7 %scatter_fusion.1 = bf16[1024,4,128]{2,1,0:T(4,128)(2,1)S(1)} fusion(bf16[1024,4,128]{2,1,0:T(4,128)(2,1)S(1)} %scatter_fusion, s32[384]{0:T(512)S(1)} %copy-done.5, bf16[384,128]{1,0:T(8,128)(2,1)S(1)} %fusion.13), kind=kCustom, calls=%fused_computation.20 | custom fusion | bytes 297984 | tf_op jit(solution)/shard_map/scatter | solution.py:144
  257.1 19.7 %scatter_fusion.2 = bf16[1024,4,128]{2,1,0:T(4,128)(2,1)S(1)} fusion(bf16[1024,4,128]{2,1,0:T(4,128)(2,1)S(1)} %scatter_fusion.1, s32[384]{0:T(512)S(1)} %copy-done.4, bf16[384,128]{1,0:T(8,128)(2,1)S(1)} %fusion.14), kind=kCustom, calls=%fused_computation.22 | custom fusion | bytes 297984 | tf_op jit(solution)/shard_map/scatter | solution.py:144
  276.8 19.6 %scatter_fusion.3 = bf16[1024,4,128]{2,1,0:T(4,128)(2,1)S(1)} fusion(bf16[1024,4,128]{2,1,0:T(4,128)(2,1)S(1)} %scatter_fusion.2, s32[384]{0:T(512)S(1)} %copy-done.3, bf16[384,128]{1,0:T(8,128)(2,1)S(1)} %fusion.15), kind=kCustom, calls=%fused_computation.24 | custom fusion | bytes 297984 | tf_op jit(solution)/shard_map/scatter | solution.py:144
  296.4 4.3 convolution_convert_fusion
  300.7 0.6 copy-done.36
  301.3 1.1 copy.70
  302.5 0.8 scatter_fusion.4
  303.3 216.1 %reduce-scatter.2.cloned.1.call-done = bf16[32,2048]{1,0:T(8,128)(2,1)} async-done(((bf16[1024,2048]{1,0:T(8,128)(2,1)}), bf16[32,2048]{1,0:T(8,128)(2,1)}) %reduce-scatter.2.cloned.1.call-update) | async-done | bytes 131088 | tf_op jit(solution)/shard_map/reduce_scatter | solution.py:146
  519.3 1.6 fusion.30
  (149 shorter events, 14.0 us)
Async XLA Ops:
  7.2 289.2 %copy-start = (bf16[512,2048]{1,0:T(8,128)(2,1)S(1)}, bf16[512,2048]{1,0:T(8,128)(2,1)}, u32[]{:S(2)}) copy-start(bf16[512,2048]{1,0:T(8,128)(2,1)} %param.15) | copy-start | bytes 6291460
  12.6 11.7 %copy-start.19 = (s32[1024,2]{0,1:T(2,128)S(1)}, s32[1024,2]{0,1:T(2,128)}, u32[]{:S(2)}) copy-start(s32[1024,2]{0,1:T(2,128)} %param.16) | copy-start | bytes 24580
  12.6 14.2 %copy-start.1 = (s32[1024]{0:T(1024)S(1)}, s32[1024]{0:T(1024)}, u32[]{:S(2)}) copy-start(s32[1024]{0:T(1024)} %param.17) | copy-start | bytes 12292
  12.6 108.8 %all-to-all-start = ((bf16[32,32,2048]{2,1,0:T(8,128)(2,1)}), bf16[32,32,2048]{2,1,0:T(8,128)(2,1)}, u32[]{:S(2)}, u32[]{:S(2)}) async-start(bf16[32,32,2048]{2,1,0:T(8,128)(2,1)} %tile.2), calls=%async_computation | async-start | bytes 8388608 | tf_op jit(solution)/shard_map/all_to_all | solution.py:98
  24.2 495.2 %reduce-scatter.2.cloned.1.call-start = ((), (), s32[]{:S(2)}) async-start(), calls=%async_computation.2 | async-start | bytes 4325376 | tf_op jit(solution)/shard_map/reduce_scatter | solution.py:146
  81.1 91.0 %copy-start.26 = (f32[64]{0:T(128)}, f32[64]{0:T(128)S(1)}, u32[]{:S(2)}) copy-start(f32[64]{0:T(128)S(1)} %multiply_power_fusion) | copy-start | bytes 772
  163.1 2.9 copy-start.12
  166.0 2.4 copy-start.16
  172.1 2.0 copy-start.21
  174.1 35.9 %collective-permute-start = (bf16[1024,128]{0,1:T(8,128)(2,1)}, bf16[1024,128]{0,1:T(8,128)(2,1)}, u32[]{:S(2)}, u32[]{:S(2)}) collective-permute-start(bf16[1024,128]{0,1:T(8,128)(2,1)} %fusion.18), channel_id=1, source_target_pairs={{0,1},{1,0},{2,3},{3,2},{4,5},{5,4},{6,7},{7,6},{8,9},{9,8},{10,11... | collective-permute-start | bytes 786440 | tf_op jit(solution)/shard_map/ppermute | solution.py:13
  177.5 13.2 %copy-start.20 = (s32[1024,2]{0,1:T(2,128)S(1)}, s32[1024,2]{0,1:T(2,128)}, u32[]{:S(2)}) copy-start(s32[1024,2]{0,1:T(2,128)} %param.16) | copy-start | bytes 24580
  177.5 13.3 %copy-start.7 = (s32[384]{0:T(512)S(1)}, s32[384]{0:T(512)}, u32[]{:S(2)}) copy-start(s32[384]{0:T(512)} %get-tuple-element.28) | copy-start | bytes 4612
  190.5 3.7 copy-start.8
  193.5 4.1 copy-start.9
  196.9 4.0 copy-start.10
  203.6 2.8 copy-start.25
  203.6 2.8 copy-start.27
  203.6 3.3 copy-start.11
  206.5 2.2 copy-start.17
  206.5 2.2 copy-start.18
  206.5 2.2 copy-start.22
  206.5 2.2 copy-start.23
  206.5 2.2 copy-start.24
  208.7 2.7 copy-start.2
  208.7 2.7 copy-start.28
  208.7 2.7 copy-start.32
  212.4 0.6 copy-start.29
  212.4 0.6 copy-start.33
  214.1 0.7 copy-start.30
  214.1 0.7 copy-start.34
  215.7 0.7 copy-start.31
  215.7 0.7 copy-start.35
  217.4 0.8 copy-start.6
  217.9 19.5 %copy-start.5 = (s32[384]{0:T(512)S(1)}, s32[384]{0:T(512)}, u32[]{:S(2)}) copy-start(s32[384]{0:T(512)} %fusion.83) | copy-start | bytes 4612
  218.2 38.9 %copy-start.4 = (s32[384]{0:T(512)S(1)}, s32[384]{0:T(512)}, u32[]{:S(2)}) copy-start(s32[384]{0:T(512)} %fusion.85) | copy-start | bytes 4612
  237.4 39.4 %copy-start.3 = (s32[384]{0:T(512)S(1)}, s32[384]{0:T(512)}, u32[]{:S(2)}) copy-start(s32[384]{0:T(512)} %fusion.87) | copy-start | bytes 4612
  300.7 0.7 copy-start.36
  300.7 1.8 copy-start.15
  300.7 218.6 %copy-start.13 = (bf16[32,2048]{1,0:T(8,128)(2,1)S(1)}, bf16[32,2048]{1,0:T(8,128)(2,1)}, u32[]{:S(2)}) copy-start(bf16[32,2048]{1,0:T(8,128)(2,1)} %param.10) | copy-start | bytes 393220
  303.3 217.7 %copy-start.14 = (bf16[16,128,128]{2,1,0:T(8,128)(2,1)}, bf16[16,128,128]{2,1,0:T(8,128)(2,1)S(1)}, u32[]{:S(2)}) copy-start(bf16[16,128,128]{2,1,0:T(8,128)(2,1)S(1)} %scatter_fusion.4) | copy-start | bytes 1572868
Sparse Core Ops, SparseCore 0:
  300.8 218.4 reduce-scatter.1
